TPU v7x, 32 devices: a whole 2x2x4 slice. The times are simulated.
32 devices in a mesh: obs: 4 (over x, core), state: 8 (over z, y).
Axes of the slice: x: 2, y: 2, z: 4, core: 2. Of those that a mesh axis runs over, the one named last changes fastest.
Arguments:
- jacobian: bfloat16 [8192, 10240], P('obs', 'state'), may hold values from -0.125 to 0.125
- obs_weight: float32 [8192], P('obs'), may hold values from 0.25 to 4
- observed: float32 [8192], P('obs'), may hold values from -6 to 6
- prior_state: bfloat16 [10240], P('state'), may hold values from -1.1953125 to 1.1953125
- prior_std: bfloat16 [10240], P('state'), may hold values from 0.5 to 2
- owner_slot: int32 [10240], P('state'), may hold values from 0 to 10239, each once
Outputs:
- gram_band: float32 [8, 1280, 3, 1280], P('state', 'obs')
- gradient: float32 [10240], P('state')
Inputs may be any that keep to these rules, and one draw needn't show every extreme that they name: owner_slot names every position once.
All inputs are finite; a program needn't handle non-finite values.
Results may differ from a plain program's by a relative error of at most 0.0028.
Values may be sent and summed in bfloat16 or wider, within the bound.
A program may use at most 128 MiB of HBM per device.

v0:
```python
import jax
import jax.numpy as jnp
from jax import lax
from jax.sharding import PartitionSpec as P


def shifted(value, axis, steps):
    count = lax.axis_size(axis)
    pairs = [(source, (source + steps) % count) for source in range(count)]
    return lax.ppermute(value, axis, pairs)


def cross_rows(left, right):
    return lax.dot_general(
        left, right, (((0,), (0,)), ((), ())), preferred_element_type=jnp.float32
    )


def on_device(jacobian, obs_weight, observed, prior_state, prior_std, owner_slot):
    width = jacobian.shape[1]
    quarter = width // lax.axis_size("obs")
    group = lax.axis_index("obs")
    weighted = (jacobian * obs_weight[:, None]).astype(jnp.bfloat16)
    spread = prior_std.astype(jnp.float32)
    rows_std = lax.dynamic_slice_in_dim(spread, group * quarter, quarter, 0)
    partial_model = jnp.dot(jacobian, prior_state, preferred_element_type=jnp.float32)
    model = lax.psum(partial_model, "state")
    misfit = (obs_weight * (observed - model)).astype(jnp.bfloat16)
    partial_descent = jnp.dot(misfit, jacobian, preferred_element_type=jnp.float32)
    descent = lax.psum(partial_descent, "obs")
    scaled = spread * descent
    next_cols, next_std = shifted((jacobian, prior_std), "state", -1)
    next_spread = next_std.astype(jnp.float32)
    far_cols, far_std = shifted((jacobian, prior_std), "state", -2)
    summed = lax.psum_scatter(
        jnp.concatenate(
            [
                cross_rows(weighted, jacobian),
                cross_rows(weighted, next_cols),
                cross_rows(weighted, far_cols),
            ],
            axis=1,
        ),
        "obs",
        scatter_dimension=0,
        tiled=True,
    )
    blocks = summed.reshape(quarter, 3, width)
    cols_std = jnp.stack([spread, next_spread, far_std.astype(jnp.float32)], axis=0)
    band = blocks * rows_std[:, None, None] * cols_std[None, :, :]
    dense = jnp.zeros((width * lax.axis_size("state"),), jnp.float32).at[owner_slot].set(scaled)
    gradient = lax.psum_scatter(dense, "state", scatter_dimension=0, tiled=True)
    return (band[None], gradient)


def solution(mesh):
    placed = (P("obs", "state"), P("obs"), P("obs"), P("state"), P("state"), P("state"))
    return jax.shard_map(
        on_device,
        mesh=mesh,
        in_specs=placed,
        out_specs=(P("state", "obs", None, None), P("state")),
        check_vma=False,
    )
```

profile of v0, /device:TPU:29, one launch (start us, length us, event | category | flops | bytes accessed | tf_op | source)
XLA Modules:
  0.0 445.7 jit_solution(2617735563554858426)
XLA Ops:
  7.2 0.0 reduce-scatter.4.cloned.1.call-start
  7.2 0.2 collective-permute-start.1
  7.5 0.2 collective-permute-start
  7.7 11.6 %fusion.2 = f32[1280,1280]{0,1:T(8,128)S(1)} fusion(bf16[2048,1280]{1,0:T(8,128)(2,1)} %param.6, f32[2048]{0:T(1024)} %param.7), kind=kOutput, calls=%fused_computation.5 | convolution fusion | flops 6718750720 | bytes 11804672 | tf_op jit(solution)/shard_map/dot_general | solution.py:14
  19.3 103.9 %collective-permute-done.1 = bf16[2048,1280]{1,0:T(8,128)(2,1)S(1)} collective-permute-done((bf16[2048,1280]{1,0:T(8,128)(2,1)}, bf16[2048,1280]{1,0:T(8,128)(2,1)S(1)}, u32[]{:S(2)}, u32[]{:S(2)}) %collective-permute-start.1) | collective-permute-done | bytes 5242912 | tf_op jit(solution)/shard_map/ppermute | solution.py:10
  123.2 7.2 %fusion = f32[1280,1280]{0,1:T(8,128)S(1)} fusion(bf16[2048,1280]{1,0:T(8,128)(2,1)S(1)} %collective-permute-done.1, bf16[2048,1280]{1,0:T(8,128)(2,1)S(1)} %copy-done, f32[2048]{0:T(1024)S(1)} %copy-done.2), kind=kOutput, calls=%fused_computation.3 | convolution fusion | flops 6718750720 | bytes 17047552 | tf_op jit(solution)/shard_map/dot_general | solution.py:14
  130.5 105.2 %collective-permute-done = bf16[2048,1280]{1,0:T(8,128)(2,1)} collective-permute-done((bf16[2048,1280]{1,0:T(8,128)(2,1)}, bf16[2048,1280]{1,0:T(8,128)(2,1)}, u32[]{:S(2)}, u32[]{:S(2)}) %collective-permute-start) | collective-permute-done | bytes 5242912 | tf_op jit(solution)/shard_map/ppermute | solution.py:10
  235.6 9.4 %fusion.1 = f32[1280,1280]{0,1:T(8,128)S(1)} fusion(bf16[2048,1280]{1,0:T(8,128)(2,1)} %collective-permute-done, bf16[2048,1280]{1,0:T(8,128)(2,1)S(1)} %copy-done, f32[2048]{0:T(1024)S(1)} %copy-done.2), kind=kOutput, calls=%fused_computation.4 | convolution fusion | flops 6718750720 | bytes 17047552 | tf_op jit(solution)/shard_map/dot_general | solution.py:14
  245.0 7.1 %pad_maximum_fusion = f32[1280,3840]{0,1:T(8,128)} fusion(f32[1280,1280]{0,1:T(8,128)S(1)} %fusion, f32[1280,1280]{0,1:T(8,128)S(1)} %fusion.1, f32[1280,1280]{0,1:T(8,128)S(1)} %fusion.2), kind=kLoop, calls=%fused_computation.1 | loop fusion | flops 9830400 | bytes 39321600 | tf_op jit(solution)/shard_map/concatenate | solution.py:36
  252.1 21.6 %copy.10 = f32[1280,3840]{1,0:T(8,128)} copy(f32[1280,3840]{0,1:T(8,128)} %pad_maximum_fusion) | data formatting | bytes 39321600
  273.8 0.7 copy-done.1
  274.5 3.9 fusion.8
  278.4 15.6 %psum.14 = f32[2048]{0:T(1024)S(1)} all-reduce(f32[2048]{0:T(1024)S(1)} %bitcast.12), channel_id=1, replica_groups=mesh['obs'=4,'state'=8] {'state'}, use_global_device_ids=true, to_apply=%region_1.0 | all-reduce | flops 2048 | bytes 16384 | tf_op jit(solution)/shard_map/psum | solution.py:27
  294.1 4.6 %convolution_reduce_fusion = f32[1280]{0:T(1024)S(1)} fusion(bf16[2048,1]{0,1:T(2,128)(2,1)S(1)} %reshape.37, bf16[2048,1280]{1,0:T(8,128)(2,1)} %param.6), kind=kOutput, calls=%fused_computation.10 | convolution fusion | flops 5242880 | bytes 5252096 | tf_op jit(solution)/shard_map/dot_general | solution.py:29
  298.6 11.1 %psum.15 = f32[1280]{0:T(1024)S(1)} all-reduce(f32[1280]{0:T(1024)S(1)} %convolution_reduce_fusion), channel_id=1, replica_groups=mesh['obs'=4,'state'=8] {'obs'}, use_global_device_ids=true, to_apply=%region_2.0 | all-reduce | flops 1280 | bytes 10240 | tf_op jit(solution)/shard_map/psum | solution.py:30
  309.8 5.3 %scatter_custom_fusion = f32[10240]{0:T(1024)S(1)} fusion(s32[1280]{0:T(1024)S(1)} %compare_select_fusion, f32[1280]{0:T(1024)S(1)} %convert_multiply_fusion, f32[]{:T(128)} %constant.4.clone.1), kind=kCustom, calls=%fused_computation.13 | custom fusion | bytes 40964 | tf_op jit(solution)/shard_map/scatter | solution.py:51
  315.1 26.1 %all-reduce = f32[10240]{0:T(1024)S(1)} all-reduce(f32[10240]{0:T(1024)S(1)} %scatter_custom_fusion), channel_id=3, replica_groups=mesh['obs'=4,'state'=8] {'state'}, use_global_device_ids=true, to_apply=%region_4.0.clone | all-reduce | flops 10240 | bytes 81920
  341.2 0.1 dynamic_slice.3
  341.3 0.6 dynamic-slice
  342.5 0.7 dynamic-slice.1
  343.2 77.0 %reduce-scatter.4.cloned.1.call-done = f32[320,3840]{1,0:T(8,128)} async-done(((f32[1280,3840]{1,0:T(8,128)}), f32[320,3840]{1,0:T(8,128)}) %reduce-scatter.4.cloned.1.call-update) | async-done | bytes 4915216
  420.3 6.1 %copy.11 = f32[320,3840]{0,1:T(8,128)} copy(f32[320,3840]{1,0:T(8,128)} %reduce-scatter.4.cloned.1.call-done) | data formatting | bytes 9830400
  426.4 7.3 %copy.9 = f32[1,320,3,1280]{3,1,2,0:T(8,128)} copy(f32[1,320,3,1280]{1,3,2,0:T(8,128)} %bitcast.11) | data formatting | bytes 9830400 | tf_op jit(solution)/shard_map/reshape | solution.py:48
  433.7 5.2 %multiply_multiply_fusion = f32[1,320,3,1280]{3,1,2,0:T(8,128)} fusion(f32[1,320,3,1280]{3,1,2,0:T(8,128)} %copy.9, f32[3,1280]{1,0:T(4,128)S(1)} %pad_maximum_fusion.1, f32[320]{0:T(512)S(1)} %dynamic_slice.3), kind=kLoop, calls=%fused_computation.9 | loop fusion | flops 2457600 | bytes 9847040 | tf_op jit(solution)/shard_map/mul | solution.py:50
  (27 shorter events, 0.1 us)
Async XLA Ops:
  7.2 116.0 %copy-start.2 = (f32[2048]{0:T(1024)S(1)}, f32[2048]{0:T(1024)}, u32[]{:S(2)}) copy-start(f32[2048]{0:T(1024)} %param.7) | copy-start | bytes 24580
  7.2 413.1 %reduce-scatter.4.cloned.1.call-start = ((), (), s32[]{:S(2)}) async-start(), calls=%async_computation.1 | async-start | bytes 24576000
  7.2 116.0 %copy-start = (bf16[2048,1280]{1,0:T(8,128)(2,1)S(1)}, bf16[2048,1280]{1,0:T(8,128)(2,1)}, u32[]{:S(2)}) copy-start(bf16[2048,1280]{1,0:T(8,128)(2,1)} %param.6) | copy-start | bytes 15728644
  7.2 116.0 %collective-permute-start.1 = (bf16[2048,1280]{1,0:T(8,128)(2,1)}, bf16[2048,1280]{1,0:T(8,128)(2,1)S(1)}, u32[]{:S(2)}, u32[]{:S(2)}) collective-permute-start(bf16[2048,1280]{1,0:T(8,128)(2,1)} %param.6), channel_id=1, source_target_pairs={{0,6},{1,7},{2,0},{3,1},{4,2},{5,3},{6,4},{7,5},{8,14},{9,15},{10,... | collective-permute-start | bytes 15728648 | tf_op jit(solution)/shard_map/ppermute | solution.py:10
  7.5 228.2 %collective-permute-start = (bf16[2048,1280]{1,0:T(8,128)(2,1)}, bf16[2048,1280]{1,0:T(8,128)(2,1)}, u32[]{:S(2)}, u32[]{:S(2)}) collective-permute-start(bf16[2048,1280]{1,0:T(8,128)(2,1)} %param.6), channel_id=1, source_target_pairs={{0,7},{1,0},{2,1},{3,2},{4,3},{5,4},{6,5},{7,6},{8,15},{9,8},{10,9... | collective-permute-start | bytes 15728648 | tf_op jit(solution)/shard_map/ppermute | solution.py:10
  273.7 0.7 copy-start.1
  273.7 0.7 copy-start.5
  274.4 19.6 %copy-start.3 = (f32[2048]{0:T(1024)S(1)}, f32[2048]{0:T(1024)}, u32[]{:S(2)}) copy-start(f32[2048]{0:T(1024)} %param.8) | copy-start | bytes 24580
  274.4 68.8 %collective-permute-start.3 = (bf16[1280]{0:T(1024)(128)(2,1)S(1)}, bf16[1280]{0:T(1024)(128)(2,1)S(1)}, u32[]{:S(2)}, u32[]{:S(2)}) collective-permute-start(bf16[1280]{0:T(1024)(128)(2,1)S(1)} %copy-done.1), channel_id=1, source_target_pairs={{0,6},{1,7},{2,0},{3,1},{4,2},{5,3},{6,4},{7,5},{8,14},{9,15},{10,... | collective-permute-start | bytes 7688 | tf_op jit(solution)/shard_map/ppermute | solution.py:10
  274.4 68.8 %collective-permute-start.2 = (bf16[1280]{0:T(1024)(128)(2,1)S(1)}, bf16[1280]{0:T(1024)(128)(2,1)S(1)}, u32[]{:S(2)}, u32[]{:S(2)}) collective-permute-start(bf16[1280]{0:T(1024)(128)(2,1)S(1)} %copy-done.1), channel_id=1, source_target_pairs={{0,7},{1,0},{2,1},{3,2},{4,3},{5,4},{6,5},{7,6},{8,15},{9,8},{10,9... | collective-permute-start | bytes 7688 | tf_op jit(solution)/shard_map/ppermute | solution.py:10
  274.4 35.4 %copy-start.4 = (s32[1280]{0:T(1024)S(1)}, s32[1280]{0:T(1024)}, u32[]{:S(2)}) copy-start(s32[1280]{0:T(1024)} %param.11) | copy-start | bytes 15364
  274.5 66.8 %copy-start.6 = (u32[32]{0:T(128)S(1)}, u32[32]{0:T(128)}, u32[]{:S(2)}) copy-start(u32[32]{0:T(128)} %constant.18) | copy-start | bytes 388
Sparse Core Ops, SparseCore 0:
  273.9 146.3 reduce-scatter.3
where the time goes:
time: 448 us; the launch traced here: 446 us
  waiting for transfers between devices  286 us (64%)
  blocking collectives  52.8 us (12%)
  local copies, waits for them, and re-layouts  42.3 us (9%)
  matrix products  36.7 us (8%)
  between operations  14.9 us (3%)
  other arithmetic  12.3 us (3%)
    ppermute x4, waiting for transfers between devices, shifted(): return lax.ppermute(value, axis, pairs)  209 us
    unnamed x2, waiting for transfers between devices  77 us
    unnamed x19, local copies, waits for them, and re-layouts  29.7 us
    dot_general x3, matrix products, cross_rows(): lax.dot_general(left, right, (((0,), (0,)), ((), ())), preferred_element_...  28.2 us
    unnamed x1, blocking collectives  26.1 us
    psum x1, blocking collectives, on_device(): model = lax.psum(partial_model, 'state')  15.6 us
    psum x1, blocking collectives, on_device(): descent = lax.psum(partial_descent, 'obs')  11.1 us
  transfers between devices with their start and end apart: 5, of which 3 were waited for; matrix products, arithmetic and copies ran while one was open for 8% of the time, Pallas kernels for 0%

commit v1 on v0

v1 whole, which is shorter than its diff:
```python
import functools

import jax
import jax.numpy as jnp
from jax import lax
from jax.experimental import pallas as pl
from jax.experimental.pallas import tpu as pltpu
from jax.sharding import PartitionSpec as P

MESH = pl.DeviceIdType.MESH
BF16 = jnp.bfloat16
F32 = jnp.float32
CHUNK = 256


def nn(left, right):
    return lax.dot_general(left, right, (((1,), (0,)), ((), ())), preferred_element_type=F32)


def nt(left, right):
    return lax.dot_general(left, right, (((1,), (1,)), ((), ())), preferred_element_type=F32)


def kernel(
    n_obs, n_state,
    jac, weight, observed, state, std_row, std_col, slot,
    band, gradient,
    cols, turned, far, near, csend, crecv, keep, xsend, xrecv,
    model, model_in, descent, descent_in, dense, dense_in, std_in,
    sem_local, sem_far, sem_near, sem_core, sem_x, sem_model, sem_descent, sem_dense, sem_std,
):
    group = lax.axis_index("obs")
    block = lax.axis_index("state")
    chunks, rows, wide = cols.shape
    quarter = band.shape[1]
    width = band.shape[2]
    units = 3 * chunks
    core = lax.rem(group, 2)
    side = group // 2
    other_core = {"obs": group + 1 - 2 * core}
    other_side = {"obs": lax.rem(group + 2, n_obs)}
    odd = lax.rem(block, 2)
    partner = {"state": block + 1 - 2 * odd}
    back_one = {"state": lax.rem(block + n_state - 1, n_state)}
    back_two = {"state": lax.rem(block + n_state - 2, n_state)}

    def remote(src, dst, sems, where, send, recv):
        return pltpu.make_async_remote_copy(
            src_ref=src, dst_ref=dst, send_sem=sems.at[0, send], recv_sem=sems.at[1, recv],
            device_id=where, device_id_type=MESH,
        )

    def local_copy(c):
        return pltpu.make_async_copy(
            jac.at[:, pl.ds(pl.multiple_of(c * wide, wide), wide)], cols.at[c], sem_local.at[c]
        )

    def far_copy(c):
        return remote(cols.at[c], far.at[c], sem_far, back_two, c, c)

    def near_copy(c, src):
        return remote(src.at[c], near.at[c], sem_near, partner, c, c)

    def core_copy(u):
        return remote(csend.at[u], crecv.at[u], sem_core, other_core, u, u)

    def side_copy(u):
        return remote(xsend.at[u], xrecv.at[u], sem_x, other_side, u, u)

    def each(count, body):
        def step(i, carry):
            body(i)
            return carry

        lax.fori_loop(0, count, step, 0)

    each(chunks, lambda c: local_copy(c).start())
    barrier = pltpu.get_barrier_semaphore()

    def greet_state(d):
        to = lax.rem(block + 1 + d, n_state)
        pl.semaphore_signal(barrier, inc=1, device_id={"state": to}, device_id_type=MESH)

    def greet_obs(d):
        to = lax.rem(group + 1 + d, n_obs)
        pl.semaphore_signal(barrier, inc=1, device_id={"obs": to}, device_id_type=MESH)

    each(n_state - 1, greet_state)
    each(n_obs - 1, greet_obs)
    pl.semaphore_wait(barrier, n_state - 1 + n_obs - 1)

    def launch(c):
        local_copy(c).wait()
        far_copy(c).start()

        @pl.when(odd == 1)
        def _():
            near_copy(c, cols).start()

    each(chunks, launch)
    std_near = remote(std_row, std_in.at[0], sem_std, back_one, 0, 0)
    std_far = remote(std_row, std_in.at[1], sem_std, back_two, 1, 1)
    std_near.start()
    std_far.start()

    parts = rows // wide

    def turn(i):
        c = i // parts
        r = pl.multiple_of(lax.rem(i, parts) * wide, wide)
        across = pl.ds(r, wide)
        down = pl.ds(pl.multiple_of(c * wide, wide), wide)
        tile = cols[c, across, :].astype(F32).T
        turned[down, across] = (tile * weight[:, across]).astype(BF16)
        lead = jnp.broadcast_to(state[:, down], (16, wide))
        piece = nn(lead, tile.astype(BF16))[:1]

        @pl.when(c == 0)
        def _():
            model[:, across] = piece

        @pl.when(c > 0)
        def _():
            model[:, across] += piece

    each(chunks * parts, turn)

    def model_copy(d):
        to = lax.rem(block + 1 + d, n_state)
        return remote(model, model_in.at[block], sem_model, {"state": to}, d, block)

    def model_landed(d):
        of = lax.rem(block + 1 + d, n_state)
        return remote(model, model_in.at[of], sem_model, {"state": of}, d, of)

    each(n_state - 1, lambda d: model_copy(d).start())

    def multiply(src, u):
        def given(h):
            q = 2 * h + 1 - core
            left = turned[pl.ds(pl.multiple_of(q * quarter, quarter), quarter), :]
            csend[u, h] = nn(left, src[...]).astype(BF16)

        def kept(h):
            q = 2 * h + core
            left = turned[pl.ds(pl.multiple_of(q * quarter, quarter), quarter), :]
            keep[u, h] = nn(left, src[...])

        each(2, given)
        core_copy(u).start()
        each(2, kept)

    def pass_on(u):
        core_copy(u).wait_recv()
        xsend[u] = (keep[u, 1 - side] + crecv[u, 1 - side].astype(F32)).astype(BF16)
        side_copy(u).start()
        keep[u, side] += crecv[u, side].astype(F32)

    my_rows = std_col[pl.ds(pl.multiple_of(group * quarter, quarter), quarter), :]

    def finish(u, k, c):
        side_copy(u).wait_recv()
        at = pl.ds(pl.multiple_of(c * wide, wide), wide)
        if k == 0:
            scale = std_row[:, at]
        else:
            scale = std_in[k - 1, :, at]
        band[k, :, at] = (keep[u, side] + xrecv[u].astype(F32)) * my_rows * scale

    def own(c):
        multiply(cols.at[c], c)

        @pl.when(c >= 1)
        def _():
            pass_on(c - 1)

        @pl.when(c >= 2)
        def _():
            finish(c - 2, 0, c - 2)

    each(chunks, own)

    def descent_copy(d):
        to = lax.rem(group + 1 + d, n_obs)
        return remote(descent, descent_in.at[group], sem_descent, {"obs": to}, d, group)

    def descent_landed(d):
        of = lax.rem(group + 1 + d, n_obs)
        return remote(descent, descent_in.at[of], sem_descent, {"obs": of}, d, of)

    def dense_copy(d):
        to = lax.rem(block + 1 + d, n_state)
        return remote(dense.at[to], dense_in.at[block], sem_dense, {"state": to}, d, block)

    def dense_landed(d):
        of = lax.rem(block + 1 + d, n_state)
        return remote(dense.at[of], dense_in.at[of], sem_dense, {"state": of}, d, of)

    def do_misfit():
        each(n_state - 1, lambda d: model_landed(d).wait_recv())
        model_in[block] = model[...]
        total = jnp.sum(model_in[...], axis=0)
        misfit = (weight[...] * (observed[...] - total)).astype(BF16)
        lead = jnp.broadcast_to(misfit, (16, rows))

        def part(c):
            at = pl.ds(pl.multiple_of(c * wide, wide), wide)
            descent[:, at] = nn(lead, cols[c])[:1]

        each(chunks, part)
        each(n_obs - 1, lambda d: descent_copy(d).start())

    def do_owners():
        each(n_obs - 1, lambda d: descent_landed(d).wait_recv())
        descent_in[group] = descent[...]
        scaled = std_row[...] * jnp.sum(descent_in[...], axis=0)
        high = scaled.astype(BF16).astype(F32)
        rest = scaled - high
        middle = rest.astype(BF16).astype(F32)
        low = rest - middle
        index = lax.broadcasted_iota(jnp.int32, (16, width), 0)
        three = jnp.where(
            index == 0, high, jnp.where(index == 1, middle, jnp.where(index == 2, low, 0.0))
        ).astype(BF16)
        place = lax.broadcasted_iota(jnp.int32, (wide, width), 0)

        def spread(i):
            t = i // chunks
            c = lax.rem(i, chunks)
            hot = jnp.where(slot[...] == place + i * wide, 1.0, 0.0).astype(BF16)
            at = pl.ds(pl.multiple_of(c * wide, wide), wide)
            dense[t, :, at] = jnp.sum(nt(three, hot), axis=0, keepdims=True)

        each(n_state * chunks, spread)
        each(n_state - 1, lambda d: dense_copy(d).start())

    def arrivals(j):
        @pl.when(j < chunks)
        def _():
            far_copy(j).wait_recv()

            @pl.when(odd == 0)
            def _():
                near_copy(j, far).start()

        @pl.when(j >= 1)
        def _():
            u = chunks + 2 * j - 1
            near_copy(j - 1, cols).wait_recv()
            multiply(near.at[j - 1], u)
            pass_on(u - 1)

            @pl.when(j >= 2)
            def _():
                finish(u - 2, 1, j - 2)

            @pl.when(j == 1)
            def _():
                finish(u - 2, 0, chunks - 1)
                std_near.wait_recv()
                std_far.wait_recv()

        @pl.when(j < chunks)
        def _():
            u = chunks + 2 * j
            multiply(far.at[j], u)
            pass_on(u - 1)

            @pl.when(j >= 1)
            def _():
                finish(u - 2, 2, j - 1)

            @pl.when(j == 0)
            def _():
                finish(u - 2, 0, chunks - 2)

        @pl.when(j == 1)
        def _():
            do_misfit()

        @pl.when(j == 2)
        def _():
            do_owners()

    each(chunks + 1, arrivals)
    pass_on(units - 1)
    each(n_state - 1, lambda d: dense_landed(d).wait_recv())
    dense_in[block] = dense[block]
    gradient[...] = jnp.sum(dense_in[...], axis=0)
    finish(units - 2, 2, chunks - 1)
    finish(units - 1, 1, chunks - 1)

    def sent(c):
        far_copy(c).wait_send()
        near_copy(c, cols).wait_send()

    each(chunks, sent)
    each(units, lambda u: core_copy(u).wait_send())
    each(units, lambda u: side_copy(u).wait_send())
    each(n_state - 1, lambda d: model_copy(d).wait_send())
    each(n_state - 1, lambda d: dense_copy(d).wait_send())
    each(n_obs - 1, lambda d: descent_copy(d).wait_send())
    std_near.wait_send()
    std_far.wait_send()


def on_device(n_obs, n_state, jacobian, obs_weight, observed, prior_state, prior_std, owner_slot):
    rows, width = jacobian.shape
    quarter = width // n_obs
    chunks = width // CHUNK
    units = 3 * chunks
    spread = prior_std.astype(F32)
    vmem = pl.BlockSpec(memory_space=pltpu.VMEM)
    dma = pltpu.SemaphoreType.DMA
    band, gradient = pl.pallas_call(
        functools.partial(kernel, n_obs, n_state),
        out_shape=(
            jax.ShapeDtypeStruct((3, quarter, width), F32),
            jax.ShapeDtypeStruct((1, width), F32),
        ),
        in_specs=[pl.BlockSpec(memory_space=pl.ANY)] + [vmem] * 6,
        out_specs=(vmem, vmem),
        scratch_shapes=[
            pltpu.VMEM((chunks, rows, CHUNK), BF16),
            pltpu.VMEM((width, rows), BF16),
            pltpu.VMEM((chunks, rows, CHUNK), BF16),
            pltpu.VMEM((chunks, rows, CHUNK), BF16),
            pltpu.VMEM((units, 2, quarter, CHUNK), BF16),
            pltpu.VMEM((units, 2, quarter, CHUNK), BF16),
            pltpu.VMEM((units, 2, quarter, CHUNK), F32),
            pltpu.VMEM((units, quarter, CHUNK), BF16),
            pltpu.VMEM((units, quarter, CHUNK), BF16),
            pltpu.VMEM((1, rows), F32),
            pltpu.VMEM((n_state, 1, rows), F32),
            pltpu.VMEM((1, width), F32),
            pltpu.VMEM((n_obs, 1, width), F32),
            pltpu.VMEM((n_state, 1, width), F32),
            pltpu.VMEM((n_state, 1, width), F32),
            pltpu.VMEM((2, 1, width), F32),
            dma((chunks,)),
            dma((2, chunks)),
            dma((2, chunks)),
            dma((2, units)),
            dma((2, units)),
            dma((2, n_state)),
            dma((2, n_obs)),
            dma((2, n_state)),
            dma((2, 2)),
        ],
        compiler_params=pltpu.CompilerParams(
            collective_id=0, has_side_effects=True, vmem_limit_bytes=60 * 1024 * 1024
        ),
        cost_estimate=pl.CostEstimate(
            flops=6 * rows * width * width, bytes_accessed=10 * rows * width, transcendentals=0
        ),
        name="band_and_gradient",
    )(
        jacobian, obs_weight[None, :], observed[None, :], prior_state[None, :],
        spread[None, :], spread[:, None], owner_slot[None, :],
    )
    return jnp.transpose(band, (1, 0, 2))[None], gradient[0]


def solution(mesh):
    n_obs, n_state = mesh.shape["obs"], mesh.shape["state"]
    assert n_obs == 4 and n_state % 2 == 0
    placed = (P("obs", "state"), P("obs"), P("obs"), P("state"), P("state"), P("state"))
    return jax.shard_map(
        functools.partial(on_device, n_obs, n_state),
        mesh=mesh,
        in_specs=placed,
        out_specs=(P("state", "obs", None, None), P("state")),
        check_vma=False,
    )
```

time: 448 us -> 218 us (0.49)
  waiting for transfers between devices: 286 us -> 0 us
  Pallas kernels: 0 us -> 203 us
  blocking collectives: 52.8 us -> 0 us
  matrix products: 36.7 us -> 0 us
  local copies, waits for them, and re-layouts: 42.3 us -> 10.6 us
  between operations: 14.9 us -> 0.64 us
  other arithmetic: 12.3 us -> 1.31 us
    ppermute x4 -> x0, waiting for transfers between devices: 209 us -> none  [shifted(): return lax.ppermute(value, axis, pairs)]
    pallas_call x0 -> x1, Pallas kernels: none -> 203 us  [on_device(): pl.pallas_call(functools.partial(kernel, n_obs, n_state), out_shape=(jax....]
    unnamed x2 -> x0, waiting for transfers between devices: 77 us -> none
    dot_general x5 -> x0, matrix products: 36.7 us -> none  [the longest x3 28.2 us: cross_rows(): lax.dot_general(left, right, (((0,), (0,)), ((), ())), preferred_element_...]
    psum x2 -> x0, blocking collectives: 26.8 us -> none  [the longest x1 15.6 us: on_device(): model = lax.psum(partial_model, 'state')]
    unnamed x1 -> x0, blocking collectives: 26.1 us -> none
    unnamed x19 -> x1, local copies, waits for them, and re-layouts: 29.7 us -> 4.96 us
    reshape x1 -> x0, local copies, waits for them, and re-layouts: 7.27 us -> none  [on_device(): blocks = summed.reshape(quarter, 3, width)]
  transfers between devices with their start and end apart: 5 -> 0, of which waited for: 3 -> 0; matrix products, arithmetic and copies ran while one was open for 8% -> 0% of each run, Pallas kernels for 0% -> 0%
where the time goes in v1:
time: 218 us; the launch traced here: 216 us
  Pallas kernels  203 us (93%)
  local copies, waits for them, and re-layouts  10.6 us (5%)
    pallas_call x1, Pallas kernels, on_device(): pl.pallas_call(functools.partial(kernel, n_obs, n_state), out_shape=(jax....  203 us
    unnamed x1, local copies, waits for them, and re-layouts  4.96 us

profile of v1, /device:TPU:29, one launch (start us, length us, event | category | flops | bytes accessed | tf_op | source)
XLA Modules:
  0.0 215.7 jit_solution(14164000254144504287)
XLA Ops:
  0.6 1.3 broadcast_in_dim.23.state
  1.9 1.3 broadcast_in_dim.26.slot
  3.2 1.3 broadcast_in_dim.24.std_row
  4.5 1.8 broadcast_in_dim.28.std_col
  6.2 203.2 %band_and_gradient.1 = (f32[3,320,1280]{2,1,0:T(8,128)}, f32[1,1280]{1,0:T(1,128)}) custom-call(bf16[2048,1280]{1,0:T(8,128)(2,1)} %jac.1, f32[1,2048]{1,0:T(1,128)} %bitcast.6, f32[1,2048]{1,0:T(1,128)} %bitcast.7, bf16[1,1280]{1,0:T(2,128)(2,1)} %broadcast_in_dim.23.state, f32[1,1280]{1,0:T(1,128)} %broadcast_in_dim.24.std_row, ...), custom_call_target="tpu_custom_call" | custom-call | flops 20132659200 | bytes 26214400 | tf_op jit(solution)/shard_map/band_and_gradient/pallas_call | solution.py:315
  209.5 1.3 reduce
  210.8 5.0 %copy.10 = f32[1,320,3,1280]{3,1,2,0:T(8,128)} copy(f32[1,320,3,1280]{3,1,2,0:T(8,128)} %bitcast.5) | data formatting | bytes 9830400

commit v2 on v1

--- a/solution.py
+++ b/solution.py
@@ -23,10 +23,10 @@
 
 def kernel(
     n_obs, n_state,
-    jac, weight, observed, state, std_row, std_col, slot,
+    jac, weight, observed, rows_in,
     band, gradient,
     cols, turned, far, near, csend, crecv, keep, xsend, xrecv,
-    model, model_in, descent, descent_in, dense, dense_in, std_in,
+    model, model_in, descent, descent_in, dense, dense_in, std_in, std_row, std_col,
     sem_local, sem_far, sem_near, sem_core, sem_x, sem_model, sem_descent, sem_dense, sem_std,
 ):
     group = lax.axis_index("obs")
@@ -75,6 +75,7 @@
         lax.fori_loop(0, count, step, 0)
 
     each(chunks, lambda c: local_copy(c).start())
+    std_row[...] = rows_in[1:2, :]
     barrier = pltpu.get_barrier_semaphore()
 
     def greet_state(d):
@@ -90,14 +91,17 @@
     pl.semaphore_wait(barrier, n_state - 1 + n_obs - 1)
 
     def launch(c):
-        local_copy(c).wait()
         far_copy(c).start()
 
         @pl.when(odd == 1)
         def _():
             near_copy(c, cols).start()
 
-    each(chunks, launch)
+    local_copy(0).wait()
+    launch(0)
+    local_copy(1).wait()
+    launch(1)
+    each(chunks - 2, lambda c: local_copy(c + 2).wait())
     std_near = remote(std_row, std_in.at[0], sem_std, back_one, 0, 0)
     std_far = remote(std_row, std_in.at[1], sem_std, back_two, 1, 1)
     std_near.start()
@@ -112,7 +116,7 @@
         down = pl.ds(pl.multiple_of(c * wide, wide), wide)
         tile = cols[c, across, :].astype(F32).T
         turned[down, across] = (tile * weight[:, across]).astype(BF16)
-        lead = jnp.broadcast_to(state[:, down], (16, wide))
+        lead = jnp.broadcast_to(rows_in[0:1, down], (16, wide)).astype(BF16)
         piece = nn(lead, tile.astype(BF16))[:1]
 
         @pl.when(c == 0)
@@ -124,6 +128,12 @@
             model[:, across] += piece
 
     each(chunks * parts, turn)
+
+    def upright(c):
+        at = pl.ds(pl.multiple_of(c * wide, wide), wide)
+        std_col[at, :] = jnp.broadcast_to(std_row[:, at], (std_col.shape[1], wide)).T
+
+    each(chunks, upright)
 
     def model_copy(d):
         to = lax.rem(block + 1 + d, n_state)
@@ -156,7 +166,7 @@
         side_copy(u).start()
         keep[u, side] += crecv[u, side].astype(F32)
 
-    my_rows = std_col[pl.ds(pl.multiple_of(group * quarter, quarter), quarter), :]
+    my_rows = std_col[pl.ds(pl.multiple_of(group * quarter, quarter), quarter), 0:1]
 
     def finish(u, k, c):
         side_copy(u).wait_recv()
@@ -166,19 +176,6 @@
         else:
             scale = std_in[k - 1, :, at]
         band[k, :, at] = (keep[u, side] + xrecv[u].astype(F32)) * my_rows * scale
-
-    def own(c):
-        multiply(cols.at[c], c)
-
-        @pl.when(c >= 1)
-        def _():
-            pass_on(c - 1)
-
-        @pl.when(c >= 2)
-        def _():
-            finish(c - 2, 0, c - 2)
-
-    each(chunks, own)
 
     def descent_copy(d):
         to = lax.rem(group + 1 + d, n_obs)
@@ -227,52 +224,65 @@
         def spread(i):
             t = i // chunks
             c = lax.rem(i, chunks)
-            hot = jnp.where(slot[...] == place + i * wide, 1.0, 0.0).astype(BF16)
+            hot = jnp.where(rows_in[2:3, :] == (place + i * wide).astype(F32), 1.0, 0.0).astype(BF16)
             at = pl.ds(pl.multiple_of(c * wide, wide), wide)
             dense[t, :, at] = jnp.sum(nt(three, hot), axis=0, keepdims=True)
 
         each(n_state * chunks, spread)
         each(n_state - 1, lambda d: dense_copy(d).start())
 
+    def of_far(c):
+        return 3 * c
+
+    def of_own(c):
+        return 3 * c + 1
+
+    def of_near(c):
+        return 3 * c + 2
+
     def arrivals(j):
-        @pl.when(j < chunks)
-        def _():
-            far_copy(j).wait_recv()
-
-            @pl.when(odd == 0)
-            def _():
-                near_copy(j, far).start()
+        far_copy(j).wait_recv()
+
+        @pl.when(odd == 0)
+        def _():
+            near_copy(j, far).start()
+
+        @pl.when(j + 2 < chunks)
+        def _():
+            launch(j + 2)
+
+        multiply(far.at[j], of_far(j))
+
+        @pl.when(j == 0)
+        def _():
+            std_near.wait_recv()
+            std_far.wait_recv()
+
+        @pl.when(j == 1)
+        def _():
+            pass_on(of_own(0))
+
+        @pl.when(j >= 2)
+        def _():
+            pass_on(of_near(j - 2))
 
         @pl.when(j >= 1)
         def _():
-            u = chunks + 2 * j - 1
+            finish(of_far(j - 1), 2, j - 1)
+
+        multiply(cols.at[j], of_own(j))
+        pass_on(of_far(j))
+
+        @pl.when(j >= 1)
+        def _():
+            finish(of_own(j - 1), 0, j - 1)
             near_copy(j - 1, cols).wait_recv()
-            multiply(near.at[j - 1], u)
-            pass_on(u - 1)
-
-            @pl.when(j >= 2)
-            def _():
-                finish(u - 2, 1, j - 2)
-
-            @pl.when(j == 1)
-            def _():
-                finish(u - 2, 0, chunks - 1)
-                std_near.wait_recv()
-                std_far.wait_recv()
-
-        @pl.when(j < chunks)
-        def _():
-            u = chunks + 2 * j
-            multiply(far.at[j], u)
-            pass_on(u - 1)
-
-            @pl.when(j >= 1)
-            def _():
-                finish(u - 2, 2, j - 1)
-
-            @pl.when(j == 0)
-            def _():
-                finish(u - 2, 0, chunks - 2)
+            multiply(near.at[j - 1], of_near(j - 1))
+            pass_on(of_own(j))
+
+        @pl.when(j >= 2)
+        def _():
+            finish(of_near(j - 2), 1, j - 2)
 
         @pl.when(j == 1)
         def _():
@@ -282,13 +292,19 @@
         def _():
             do_owners()
 
-    each(chunks + 1, arrivals)
-    pass_on(units - 1)
+    each(chunks, arrivals)
+    last = chunks - 1
+    pass_on(of_near(last - 1))
+    finish(of_far(last), 2, last)
+    finish(of_own(last), 0, last)
     each(n_state - 1, lambda d: dense_landed(d).wait_recv())
     dense_in[block] = dense[block]
     gradient[...] = jnp.sum(dense_in[...], axis=0)
-    finish(units - 2, 2, chunks - 1)
-    finish(units - 1, 1, chunks - 1)
+    near_copy(last, cols).wait_recv()
+    multiply(near.at[last], of_near(last))
+    finish(of_near(last - 1), 1, last - 1)
+    pass_on(of_near(last))
+    finish(of_near(last), 1, last)
 
     def sent(c):
         far_copy(c).wait_send()
@@ -309,7 +325,6 @@
     quarter = width // n_obs
     chunks = width // CHUNK
     units = 3 * chunks
-    spread = prior_std.astype(F32)
     vmem = pl.BlockSpec(memory_space=pltpu.VMEM)
     dma = pltpu.SemaphoreType.DMA
     band, gradient = pl.pallas_call(
@@ -318,7 +333,7 @@
             jax.ShapeDtypeStruct((3, quarter, width), F32),
             jax.ShapeDtypeStruct((1, width), F32),
         ),
-        in_specs=[pl.BlockSpec(memory_space=pl.ANY)] + [vmem] * 6,
+        in_specs=[pl.BlockSpec(memory_space=pl.ANY)] + [vmem] * 3,
         out_specs=(vmem, vmem),
         scratch_shapes=[
             pltpu.VMEM((chunks, rows, CHUNK), BF16),
@@ -337,6 +352,8 @@
             pltpu.VMEM((n_state, 1, width), F32),
             pltpu.VMEM((n_state, 1, width), F32),
             pltpu.VMEM((2, 1, width), F32),
+            pltpu.VMEM((1, width), F32),
+            pltpu.VMEM((width, 128), F32),
             dma((chunks,)),
             dma((2, chunks)),
             dma((2, chunks)),
@@ -355,8 +372,8 @@
         ),
         name="band_and_gradient",
     )(
-        jacobian, obs_weight[None, :], observed[None, :], prior_state[None, :],
-        spread[None, :], spread[:, None], owner_slot[None, :],
+        jacobian, obs_weight[None, :], observed[None, :],
+        jnp.stack([prior_state.astype(F32), prior_std.astype(F32), owner_slot.astype(F32)]),
     )
     return jnp.transpose(band, (1, 0, 2))[None], gradient[0]
 

time: 218 us -> 211 us (0.968)
  local copies, waits for them, and re-layouts: 10.6 us -> 6.35 us
    broadcast_in_dim x4 -> x0, local copies, waits for them, and re-layouts: 5.62 us -> none  [the longest x1 1.76 us: on_device(): spread[:, None]]
where the time goes in v2:
time: 211 us
  Pallas kernels  201 us (95%)
  local copies, waits for them, and re-layouts  6.35 us (3%)
  other arithmetic  2.63 us (1%)
    pallas_call x1, Pallas kernels, on_device(): pl.pallas_call(functools.partial(kernel, n_obs, n_state), out_shape=(jax....  201 us
    unnamed x1, local copies, waits for them, and re-layouts  4.96 us

profile of v2, /device:TPU:29, one launch (start us, length us, event | category | flops | bytes accessed | tf_op | source)
XLA Modules:
  0.0 210.9 jit_solution(6700443712380905461)
XLA Ops:
  0.6 0.7 reshape.4
  1.3 0.7 reshape.5
  2.0 0.7 convert_element_type.2
  2.7 0.6 pad_maximum_fusion.rows_in
  3.3 201.3 %band_and_gradient.1 = (f32[3,320,1280]{2,1,0:T(8,128)}, f32[1,1280]{1,0:T(1,128)}) custom-call(bf16[2048,1280]{1,0:T(8,128)(2,1)} %jac.1, f32[1,2048]{1,0:T(1,128)} %bitcast.6, f32[1,2048]{1,0:T(1,128)} %bitcast.7, f32[3,1280]{1,0:T(4,128)} %pad_maximum_fusion.rows_in), custom_call_target="tpu_custom_call" | custom-call | flops 20132659200 | bytes 26214400 | tf_op jit(solution)/shard_map/band_and_gradient/pallas_call | solution.py:330
  204.6 1.3 reduce
  205.9 5.0 %copy.9 = f32[1,320,3,1280]{3,1,2,0:T(8,128)} copy(f32[1,320,3,1280]{3,1,2,0:T(8,128)} %bitcast.5) | data formatting | bytes 9830400
  (1 shorter events, 0.0 us)

commit v3 on v2

--- a/solution.py
+++ b/solution.py
@@ -247,9 +247,6 @@
         def _():
             near_copy(j, far).start()
 
-        @pl.when(j + 2 < chunks)
-        def _():
-            launch(j + 2)
 
         multiply(far.at[j], of_far(j))
 
@@ -269,6 +266,11 @@
         @pl.when(j >= 1)
         def _():
             finish(of_far(j - 1), 2, j - 1)
+
+        @pl.when(j + 4 < chunks)
+        def _():
+            far_copy(j + 2).wait_send()
+            launch(j + 4)
 
         multiply(cols.at[j], of_own(j))
         pass_on(of_far(j))
@@ -284,14 +286,16 @@
         def _():
             finish(of_near(j - 2), 1, j - 2)
 
-        @pl.when(j == 1)
-        def _():
-            do_misfit()
-
-        @pl.when(j == 2)
+        @pl.when(j == 0)
         def _():
             do_owners()
 
+    def follow(c):
+        far_copy(c).wait_send()
+        launch(c + 2)
+
+    do_misfit()
+    each(2, follow)
     each(chunks, arrivals)
     last = chunks - 1
     pass_on(of_near(last - 1))
@@ -307,10 +311,11 @@
     finish(of_near(last), 1, last)
 
     def sent(c):
-        far_copy(c).wait_send()
         near_copy(c, cols).wait_send()
 
     each(chunks, sent)
+    far_copy(chunks - 2).wait_send()
+    far_copy(chunks - 1).wait_send()
     each(units, lambda u: core_copy(u).wait_send())
     each(units, lambda u: side_copy(u).wait_send())
     each(n_state - 1, lambda d: model_copy(d).wait_send())

time: 211 us -> 206 us (0.976)
  Pallas kernels: 201 us -> 196 us
    pallas_call x1, Pallas kernels: 201 us -> 196 us  [on_device(): pl.pallas_call(functools.partial(kernel, n_obs, n_state), out_shape=(jax....]
where the time goes in v3:
time: 206 us; the launch traced here: 205 us
  Pallas kernels  196 us (95%)
  local copies, waits for them, and re-layouts  6.35 us (3%)
  other arithmetic  2.63 us (1%)
    pallas_call x1, Pallas kernels, on_device(): pl.pallas_call(functools.partial(kernel, n_obs, n_state), out_shape=(jax....  196 us
    unnamed x1, local copies, waits for them, and re-layouts  4.96 us

profile of v3, /device:TPU:29, one launch (start us, length us, event | category | flops | bytes accessed | tf_op | source)
XLA Modules:
  0.0 205.3 jit_solution(14674049152816294987)
XLA Ops:
  0.6 0.7 reshape.4
  1.3 0.7 reshape.5
  2.0 0.7 convert_element_type.2
  2.7 0.6 pad_maximum_fusion.rows_in
  3.3 195.6 %band_and_gradient.1 = (f32[3,320,1280]{2,1,0:T(8,128)}, f32[1,1280]{1,0:T(1,128)}) custom-call(bf16[2048,1280]{1,0:T(8,128)(2,1)} %jac.1, f32[1,2048]{1,0:T(1,128)} %bitcast.6, f32[1,2048]{1,0:T(1,128)} %bitcast.7, f32[3,1280]{1,0:T(4,128)} %pad_maximum_fusion.rows_in), custom_call_target="tpu_custom_call" | custom-call | flops 20132659200 | bytes 26214400 | tf_op jit(solution)/shard_map/band_and_gradient/pallas_call | solution.py:335
  199.0 1.3 reduce
  200.3 5.0 %copy.9 = f32[1,320,3,1280]{3,1,2,0:T(8,128)} copy(f32[1,320,3,1280]{3,1,2,0:T(8,128)} %bitcast.5) | data formatting | bytes 9830400
  (1 shorter events, 0.0 us)

commit v4 on v2

--- a/solution.py
+++ b/solution.py
@@ -100,7 +100,6 @@
     local_copy(0).wait()
     launch(0)
     local_copy(1).wait()
-    launch(1)
     each(chunks - 2, lambda c: local_copy(c + 2).wait())
     std_near = remote(std_row, std_in.at[0], sem_std, back_one, 0, 0)
     std_far = remote(std_row, std_in.at[1], sem_std, back_two, 1, 1)
@@ -241,15 +240,18 @@
         return 3 * c + 2
 
     def arrivals(j):
+        far_copy(j).wait_send()
+
+        @pl.when(j + 1 < chunks)
+        def _():
+            launch(j + 1)
+
         far_copy(j).wait_recv()
 
         @pl.when(odd == 0)
         def _():
             near_copy(j, far).start()
 
-        @pl.when(j + 2 < chunks)
-        def _():
-            launch(j + 2)
 
         multiply(far.at[j], of_far(j))
 
@@ -284,11 +286,11 @@
         def _():
             finish(of_near(j - 2), 1, j - 2)
 
+        @pl.when(j == 0)
+        def _():
+            do_misfit()
+
         @pl.when(j == 1)
-        def _():
-            do_misfit()
-
-        @pl.when(j == 2)
         def _():
             do_owners()
 
@@ -307,7 +309,6 @@
     finish(of_near(last), 1, last)
 
     def sent(c):
-        far_copy(c).wait_send()
         near_copy(c, cols).wait_send()
 
     each(chunks, sent)

time: 211 us -> 231 us (1.095)
  Pallas kernels: 201 us -> 221 us
    pallas_call x1, Pallas kernels: 201 us -> 221 us  [on_device(): pl.pallas_call(functools.partial(kernel, n_obs, n_state), out_shape=(jax....]
where the time goes in v4:
time: 231 us
  Pallas kernels  221 us (96%)
  local copies, waits for them, and re-layouts  6.35 us (3%)
  other arithmetic  2.63 us (1%)
    pallas_call x1, Pallas kernels, on_device(): pl.pallas_call(functools.partial(kernel, n_obs, n_state), out_shape=(jax....  221 us
    unnamed x1, local copies, waits for them, and re-layouts  4.96 us

profile of v4, /device:TPU:29, one launch (start us, length us, event | category | flops | bytes accessed | tf_op | source)
XLA Modules:
  0.0 231.0 jit_solution(12493018296631837551)
XLA Ops:
  0.6 0.7 reshape.4
  1.3 0.7 reshape.5
  2.0 0.7 convert_element_type.2
  2.7 0.6 pad_maximum_fusion.rows_in
  3.3 221.4 %band_and_gradient.1 = (f32[3,320,1280]{2,1,0:T(8,128)}, f32[1,1280]{1,0:T(1,128)}) custom-call(bf16[2048,1280]{1,0:T(8,128)(2,1)} %jac.1, f32[1,2048]{1,0:T(1,128)} %bitcast.6, f32[1,2048]{1,0:T(1,128)} %bitcast.7, f32[3,1280]{1,0:T(4,128)} %pad_maximum_fusion.rows_in), custom_call_target="tpu_custom_call" | custom-call | flops 20132659200 | bytes 26214400 | tf_op jit(solution)/shard_map/band_and_gradient/pallas_call | solution.py:331
  224.7 1.3 reduce
  226.1 5.0 %copy.9 = f32[1,320,3,1280]{3,1,2,0:T(8,128)} copy(f32[1,320,3,1280]{3,1,2,0:T(8,128)} %bitcast.5) | data formatting | bytes 9830400
  (1 shorter events, 0.0 us)

commit v5 on v3

--- a/solution.py
+++ b/solution.py
@@ -241,6 +241,11 @@
         return 3 * c + 2
 
     def arrivals(j):
+        @pl.when(jnp.logical_and(j >= 2, j + 2 < chunks))
+        def _():
+            far_copy(j).wait_send()
+            launch(j + 2)
+
         far_copy(j).wait_recv()
 
         @pl.when(odd == 0)
@@ -266,11 +271,6 @@
         @pl.when(j >= 1)
         def _():
             finish(of_far(j - 1), 2, j - 1)
-
-        @pl.when(j + 4 < chunks)
-        def _():
-            far_copy(j + 2).wait_send()
-            launch(j + 4)
 
         multiply(cols.at[j], of_own(j))
         pass_on(of_far(j))

time: 206 us -> 190 us (0.922)
  Pallas kernels: 196 us -> 180 us
    pallas_call x1, Pallas kernels: 196 us -> 180 us  [on_device(): pl.pallas_call(functools.partial(kernel, n_obs, n_state), out_shape=(jax....]
where the time goes in v5:
time: 190 us
  Pallas kernels  180 us (95%)
  local copies, waits for them, and re-layouts  6.35 us (3%)
  other arithmetic  2.63 us (1%)
    pallas_call x1, Pallas kernels, on_device(): pl.pallas_call(functools.partial(kernel, n_obs, n_state), out_shape=(jax....  180 us
    unnamed x1, local copies, waits for them, and re-layouts  4.96 us

profile of v5, /device:TPU:29, one launch (start us, length us, event | category | flops | bytes accessed | tf_op | source)
XLA Modules:
  0.0 189.9 jit_solution(7364514532878058406)
XLA Ops:
  0.6 0.7 reshape.4
  1.3 0.7 reshape.5
  2.0 0.7 convert_element_type.2
  2.7 0.6 pad_maximum_fusion.rows_in
  3.3 180.3 %band_and_gradient.1 = (f32[3,320,1280]{2,1,0:T(8,128)}, f32[1,1280]{1,0:T(1,128)}) custom-call(bf16[2048,1280]{1,0:T(8,128)(2,1)} %jac.1, f32[1,2048]{1,0:T(1,128)} %bitcast.6, f32[1,2048]{1,0:T(1,128)} %bitcast.7, f32[3,1280]{1,0:T(4,128)} %pad_maximum_fusion.rows_in), custom_call_target="tpu_custom_call" | custom-call | flops 20132659200 | bytes 26214400 | tf_op jit(solution)/shard_map/band_and_gradient/pallas_call | solution.py:335
  183.6 1.3 reduce
  184.9 5.0 %copy.9 = f32[1,320,3,1280]{3,1,2,0:T(8,128)} copy(f32[1,320,3,1280]{3,1,2,0:T(8,128)} %bitcast.5) | data formatting | bytes 9830400
  (1 shorter events, 0.0 us)
